TPU v7x, 512 devices: a whole 4x8x8 slice. The times are simulated.
512 devices in a mesh: terms: 16 (over y, core), sectors: 32 (over z, x).
Axes of the slice: x: 4, y: 8, z: 8, core: 2. Of those that a mesh axis runs over, the one named last changes fastest.
Arguments:
- wavefunction: bfloat16 [4096, 4096], P('terms', 'sectors')
- left_env: bfloat16 [32, 32, 128, 128], P('terms', 'sectors')
- right_env: bfloat16 [32, 32, 128, 128], P('terms', 'sectors')
- sector_size: int32 [32], replicated, may hold values from 64 to 128, as said below
Outputs:
- sigma_first: bfloat16 [4096, 4096], P('terms', 'sectors')
- sigma_second: bfloat16 [4096, 4096], P('terms', 'sectors')
Inputs may be any that keep to these rules, and one draw needn't show every extreme that they name: `sector_size`: each block has between 64 and 128 live states; some block has exactly 128.
All inputs are finite; a program needn't handle non-finite values.
Results may differ from a plain program's by a relative error of at most 0.0069.
Values may be sent and summed in bfloat16 or wider, within the bound.
A program may use at most 64 MiB of HBM per device.

v0:
```python
import jax
import jax.numpy as jnp
from jax import lax
from jax.sharding import PartitionSpec as P


def shards(wavefunction, left_env, right_env, sector_size):
    block = left_env.shape[2]
    row_count = wavefunction.shape[0]
    col_count = wavefunction.shape[1]
    sec_local = left_env.shape[1]
    states = jnp.arange(block, dtype=jnp.int32)
    live = (states[None, :] < sector_size[:, None]).reshape(-1)
    full_dim = live.shape[0]
    term_index = lax.axis_index("terms")
    sector_index = lax.axis_index("sectors")
    row_live = lax.dynamic_slice_in_dim(live, term_index * row_count, row_count)
    col_live = lax.dynamic_slice_in_dim(live, sector_index * col_count, col_count)
    both_live = row_live[:, None] & col_live[None, :]

    def apply_ham(masked):
        column_part = lax.all_gather(masked, "terms", axis=0, tiled=True)
        row_part = lax.all_to_all(column_part, "sectors", split_axis=0, concat_axis=1, tiled=True)
        row_blocks = row_part.reshape(sec_local, block, full_dim)
        image = jnp.einsum(
            "wrab,rbc->wrac", left_env, row_blocks, preferred_element_type=jnp.float32
        )
        image = image.astype(jnp.bfloat16).reshape(left_env.shape[0], col_count, full_dim)
        image_cols = lax.all_to_all(image, "sectors", split_axis=2, concat_axis=1, tiled=True)
        image_cols = image_cols.reshape(left_env.shape[0], full_dim, sec_local, block)
        partial_sum = jnp.einsum(
            "winb,wnob->ino", image_cols, right_env, preferred_element_type=jnp.float32
        )
        partial_sum = partial_sum.reshape(full_dim, col_count)
        shared = lax.psum_scatter(partial_sum, "terms", scatter_dimension=0, tiled=True)
        return jnp.where(both_live, shared, jnp.zeros_like(shared)).astype(jnp.bfloat16)

    start = jnp.where(both_live, wavefunction, jnp.zeros_like(wavefunction))
    sigma_first = apply_ham(start)
    start_wide = start.astype(jnp.float32)
    first_wide = sigma_first.astype(jnp.float32)
    numerator, denominator = lax.psum(
        (jnp.sum(start_wide * first_wide), jnp.sum(start_wide * start_wide)), ("terms", "sectors")
    )
    theta = numerator / denominator
    correction = (first_wide - theta * start_wide).astype(jnp.bfloat16)
    sigma_second = apply_ham(correction)
    return (sigma_first, sigma_second)


def solution(mesh):
    return jax.shard_map(
        shards,
        mesh=mesh,
        in_specs=(
            P("terms", "sectors"),
            P("terms", "sectors", None, None),
            P("terms", "sectors", None, None),
            P(),
        ),
        out_specs=(P("terms", "sectors"), P("terms", "sectors")),
        check_vma=False,
    )
```

profile of v0, /device:TPU:6, one launch (start us, length us, event | category | flops | bytes accessed | tf_op | source)
XLA Modules:
  0.0 556.4 jit_solution(10549147195978146766)
XLA Ops:
  7.2 0.7 fusion.11
  8.1 1.6 and_select_fusion.2
  9.8 46.4 %all-gather.3.cloned.1.call-done = bf16[4096,128]{1,0:T(8,128)(2,1)} async-done(((bf16[256,128]{1,0:T(8,128)(2,1)}), bf16[4096,128]{1,0:T(8,128)(2,1)}) %all-gather.3.cloned.1.call-update) | async-done | bytes 1048592 | tf_op jit(solution)/shard_map/all_gather | solution.py:22
  56.2 1.6 copy.10
  57.8 38.8 %all_to_all.62 = bf16[32,128,128]{1,2,0:T(8,128)(2,1)S(1)} all-to-all(bf16[32,128,128]{1,2,0:T(8,128)(2,1)S(1)} %copy.10), channel_id=1, replica_groups=mesh['terms'=16,'sectors'=32] {'sectors'}, dimensions={0} | all-to-all | bytes 2097152 | tf_op jit(solution)/shard_map/all_to_all | solution.py:23
  96.6 0.7 fusion
  97.3 17.8 %copy.11 = bf16[2,128,4096]{1,0,2:T(2,128)(2,1)S(1)} copy(bf16[2,128,4096]{1,2,0:T(8,128)(2,1)S(1)} %fusion) | data formatting | bytes 4194304 | tf_op jit(solution)/shard_map/reshape | solution.py:28
  115.1 55.0 %all_to_all.63 = bf16[2,128,4096]{1,0,2:T(2,128)(2,1)} all-to-all(bf16[2,128,4096]{1,0,2:T(2,128)(2,1)S(1)} %copy.11), channel_id=1, replica_groups=mesh['terms'=16,'sectors'=32] {'sectors'}, dimensions={2} | all-to-all | bytes 4194304 | tf_op jit(solution)/shard_map/all_to_all | solution.py:29
  170.1 4.9 copy.12
  175.1 2.0 convolution_bitcast_fusion.1
  177.2 55.9 %reduce-scatter.3.cloned.1.call-done = f32[256,128]{1,0:T(8,128)} async-done(((f32[4096,128]{1,0:T(8,128)}), f32[256,128]{1,0:T(8,128)}) %reduce-scatter.3.cloned.1.call-update) | async-done | bytes 131088 | tf_op jit(solution)/shard_map/reduce_scatter | solution.py:35
  233.1 1.7 fusion.4
  234.7 96.6 %all-reduce = (f32[]{:T(128)}, f32[]{:T(128)}) all-reduce(f32[]{:T(128)} %get-tuple-element.3, f32[]{:T(128)} %get-tuple-element.2), channel_id=1, replica_groups=mesh['terms'=16,'sectors'=32] {'terms','sectors'}, use_global_device_ids=true, to_apply=%region_2.3 | all-reduce | flops 2 | bytes 16 | tf_op jit(solution)/shard_map/psum | solution.py:42
  332.6 0.7 fusion.2
  333.4 38.7 %all-gather.5.cloned.1.call-done = bf16[4096,128]{1,0:T(8,128)(2,1)} async-done(((bf16[256,128]{1,0:T(8,128)(2,1)}), bf16[4096,128]{1,0:T(8,128)(2,1)}) %all-gather.5.cloned.1.call-update) | async-done | bytes 1048592 | tf_op jit(solution)/shard_map/all_gather | solution.py:22
  372.1 39.0 %all_to_all.64 = bf16[32,128,128]{2,1,0:T(8,128)(2,1)S(1)} all-to-all(bf16[32,128,128]{2,1,0:T(8,128)(2,1)} %bitcast.59), channel_id=1, replica_groups=mesh['terms'=16,'sectors'=32] {'sectors'}, dimensions={0} | all-to-all | bytes 2097152 | tf_op jit(solution)/shard_map/all_to_all | solution.py:23
  411.1 0.7 copy.13
  411.8 0.7 fusion.1
  412.5 17.8 %copy.14 = bf16[2,128,4096]{1,0,2:T(2,128)(2,1)S(1)} copy(bf16[2,128,4096]{1,2,0:T(8,128)(2,1)S(1)} %fusion.1) | data formatting | bytes 4194304 | tf_op jit(solution)/shard_map/reshape | solution.py:28
  430.3 55.0 %all_to_all.65 = bf16[2,128,4096]{1,0,2:T(2,128)(2,1)} all-to-all(bf16[2,128,4096]{1,0,2:T(2,128)(2,1)S(1)} %copy.14), channel_id=1, replica_groups=mesh['terms'=16,'sectors'=32] {'sectors'}, dimensions={2} | all-to-all | bytes 4194304 | tf_op jit(solution)/shard_map/all_to_all | solution.py:29
  485.4 4.9 copy.15
  490.3 2.0 convolution_bitcast_fusion
  492.3 55.9 %reduce-scatter.5.cloned.1.call-done = f32[256,128]{1,0:T(8,128)} async-done(((f32[4096,128]{1,0:T(8,128)}), f32[256,128]{1,0:T(8,128)}) %reduce-scatter.5.cloned.1.call-update) | async-done | bytes 131088 | tf_op jit(solution)/shard_map/reduce_scatter | solution.py:35
  548.2 1.6 fusion.6
  (18 shorter events, 0.4 us)
Async XLA Ops:
  7.2 89.4 %copy-start = (bf16[2,1,128,128]{3,2,1,0:T(8,128)(2,1)S(1)}, bf16[2,1,128,128]{3,2,1,0:T(8,128)(2,1)}, u32[]{:S(2)}) copy-start(bf16[2,1,128,128]{3,2,1,0:T(8,128)(2,1)} %param.5) | copy-start | bytes 196612
  7.2 49.0 %all-gather.3.cloned.1.call-start = ((), (), s32[]{:S(2)}) async-start(), calls=%async_computation.6 | async-start | bytes 1114112 | tf_op jit(solution)/shard_map/all_gather | solution.py:22
  9.7 223.3 %reduce-scatter.3.cloned.1.call-start = ((), (), s32[]{:S(2)}) async-start(), calls=%async_computation.7 | async-start | bytes 2228224 | tf_op jit(solution)/shard_map/reduce_scatter | solution.py:35
  170.1 4.9 copy-start.2
  177.1 55.9 %copy-start.1 = (bf16[256,128]{1,0:T(8,128)(2,1)S(1)}, bf16[256,128]{1,0:T(8,128)(2,1)}, u32[]{:S(2)}) copy-start(bf16[256,128]{1,0:T(8,128)(2,1)} %param.4) | copy-start | bytes 196612
  177.1 195.0 %all-gather.5.cloned.1.call-start = ((), (), s32[]{:S(2)}) async-start(), calls=%async_computation.8 | async-start | bytes 1114112 | tf_op jit(solution)/shard_map/all_gather | solution.py:22
  234.7 177.1 %copy-start.3 = (bf16[256,128]{1,0:T(8,128)(2,1)}, bf16[256,128]{1,0:T(8,128)(2,1)S(1)}, u32[]{:S(2)}) copy-start(bf16[256,128]{1,0:T(8,128)(2,1)S(1)} %get-tuple-element.6) | copy-start | bytes 196612
  333.4 214.9 %reduce-scatter.5.cloned.1.call-start = ((), (), s32[]{:S(2)}) async-start(), calls=%async_computation.9 | async-start | bytes 2228224 | tf_op jit(solution)/shard_map/reduce_scatter | solution.py:35
Sparse Core Ops, SparseCore 0:
  10.7 45.4 all-gather.2
  177.3 55.7 reduce-scatter.2
  333.5 38.6 all-gather.4
  492.4 55.7 reduce-scatter.4
where the time goes:
time: 557 us; the launch traced here: 556 us
  blocking collectives  284 us (51%)
  waiting for transfers between devices  197 us (35%)
  local copies, waits for them, and re-layouts  47.9 us (9%)
  between operations  15.2 us (3%)
  other arithmetic  6.33 us (1%)
    reduce_scatter x2, waiting for transfers between devices, apply_ham(): lax.psum_scatter(partial_sum, 'terms', scatter_dimension=0, tiled=True)  112 us
    all_to_all x2, blocking collectives, apply_ham(): lax.all_to_all(image, 'sectors', split_axis=2, concat_axis=1, tiled=True)  110 us
    psum x1, blocking collectives, shards(): lax.psum((jnp.sum(start_wide * first_wide), jnp.sum(start_wide * start_wi...  96.6 us
    all_gather x2, waiting for transfers between devices, apply_ham(): column_part = lax.all_gather(masked, 'terms', axis=0, tiled=True)  85.1 us
    all_to_all x2, blocking collectives, apply_ham(): lax.all_to_all(column_part, 'sectors', split_axis=0, concat_axis=1, tiled...  77.7 us
    reshape x2, local copies, waits for them, and re-layouts, apply_ham(): image.astype(jnp.bfloat16).reshape(left_env.shape[0], col_count, full_dim)  35.6 us
  transfers between devices with their start and end apart: 4, of which 4 were waited for; matrix products, arithmetic and copies ran while one was open for 0% of the time, Pallas kernels for 0%

commit v1 on v0

v1 whole, which is shorter than its diff:
```python
import functools

import jax
import jax.numpy as jnp
from jax import lax
from jax.experimental import pallas as pl
from jax.experimental.pallas import tpu as pltpu
from jax.sharding import PartitionSpec as P

MESH = pl.DeviceIdType.MESH
BLK = 128
X, Y, Z = 4, 8, 8
OFFS = (0, -1, 1, -2, 2, -3, 3, 4)


def wrap(value, n):
    return lax.rem(value + 2 * n, n)


def device(x, y, z, c):
    return {"terms": 2 * y + c, "sectors": 4 * z + x}


def kernel(
    size_ref, v_hbm, l_hbm, r_hbm, out1, out2,
    lb, rz, rb, vt, vc, im, s1, g, s1h, gh, part, core_in, x_in, y_in, z_in,
    local_sem, lring_s, lring_r, lx_s, lx_r, ld_s, ld_r, lf_s, lf_r,
    rring_s, rring_r, ra_s, ra_r, rd_s, rd_r, vs, vr, vfs, vfr, hs, hr, ts, tr,
):
    t, s = lax.axis_index("terms"), lax.axis_index("sectors")
    y, c = t // 2, lax.rem(t, 2)
    z, x = s // 4, lax.rem(s, 4)
    other = 1 - c
    ct = x // 2
    own = c == ct
    slot = jnp.where(own, lax.rem(x, 2), 2)
    same_row = lax.rem(x, 2)
    near_row = 1 - same_row
    outer = jnp.logical_or(x == 0, x == 3)
    near = jnp.where(outer != (c == 1), 1, -1)
    diag = y == z

    barrier = pltpu.get_barrier_semaphore()
    peers = [device(x, y, z, other)]
    for dx in (1, 2, 3):
        for e in (0, 1):
            peers.append(device(wrap(x + dx, X), y, z, e))
    for d in range(1, 8):
        peers.append(device(x, wrap(y + d, Y), z, c))
        peers.append(device(x, y, wrap(z + d, Z), c))
    for p in peers:
        pl.semaphore_signal(barrier, inc=1, device_id=p, device_id_type=MESH)
    pl.semaphore_wait(barrier, len(peers))

    sent = []

    def send(src, dst, ssem, rsem, to, when=None):
        cp = pltpu.make_async_remote_copy(
            src_ref=src, dst_ref=dst, send_sem=ssem, recv_sem=rsem, device_id=to, device_id_type=MESH
        )
        if when is None:
            cp.start()
        else:
            pl.when(when)(lambda: cp.start())
        sent.append((cp, when))

    def got(dst, rsem, when=None):
        cp = pltpu.make_async_remote_copy(
            src_ref=dst, dst_ref=dst, send_sem=rsem, recv_sem=rsem,
            device_id=device(x, y, z, other), device_id_type=MESH,
        )
        if when is None:
            cp.wait_recv()
        else:
            pl.when(when)(lambda: cp.wait_recv())

    yq = [wrap(y + o, Y) for o in OFFS]
    zq = [wrap(z + o, Z) for o in OFFS]
    wl = [4 * v + 2 * c for v in yq]

    def mine(q):
        return l_hbm if q == 0 else lb.at[slot, pl.ds(wl[q], 2)]

    def spread_l(q):
        src = mine(q)
        dst = lb.at[same_row, pl.ds(wl[q], 2)]
        for e, dx in enumerate((1, -1)):
            send(src, dst, lx_s.at[q, e], lx_r.at[q, c], device(wrap(x + dx, X), y, z, ct))
        send(src, dst, ld_s.at[q], ld_r.at[q], device(x, y, z, other), when=jnp.logical_not(own))

    def ring_l(q, up, to_q):
        src, w = mine(q), wl[q]
        to = device(x, wrap(y + (1 if up else -1), Y), z, c)
        if to_q < 7:
            send(src, lb.at[slot, pl.ds(w, 2)], lring_s.at[to_q], lring_r.at[to_q], to)
        else:
            i = 0 if up else 1
            send(lb.at[slot, w + i], lb.at[slot, w + i], lring_s.at[7 + i], lring_r.at[7 + i], to)

    def got_ring_l(q):
        if q < 7:
            got(lb.at[slot, pl.ds(wl[q], 2)], lring_r.at[q])
        else:
            for i in (0, 1):
                got(lb.at[slot, wl[q] + i], lring_r.at[7 + i])

    def piece_r(q):
        return r_hbm if q == 0 else rz.at[zq[q]]

    def ring_r(q, up, to_q):
        to = device(x, y, wrap(z + (1 if up else -1), Z), c)
        if to_q < 7:
            send(piece_r(q), rz.at[zq[q]], rring_s.at[to_q], rring_r.at[to_q], to)
        else:
            i = 0 if up else 1
            send(rz.at[zq[q], i], rz.at[zq[q], i], rring_s.at[7 + i], rring_r.at[7 + i], to)

    def got_ring_r(q):
        if q < 7:
            got(rz.at[zq[q]], rring_r.at[q])
        else:
            for i in (0, 1):
                got(rz.at[zq[q], i], rring_r.at[7 + i])

    w_own = 4 * y + 2 * c

    def spread_r(q):
        here = zq[q] == y
        send(
            piece_r(q), rb.at[pl.ds(w_own, 2)], ra_s.at[q], ra_r.at[y],
            device(x, zq[q], z, c), when=jnp.logical_not(here),
        )
        cp = pltpu.make_async_copy(piece_r(q), rb.at[pl.ds(w_own, 2)], local_sem.at[1])
        pl.when(here)(lambda: cp.start())

    ring_l(0, True, 1)
    ring_l(0, False, 2)
    ring_r(0, True, 1)
    ring_r(0, False, 2)
    send(v_hbm, vt.at[z], vs.at[0], vr.at[z], device(x, y, y, c), when=jnp.logical_not(diag))
    spread_l(0)
    spread_r(0)
    own_l = pltpu.make_async_copy(l_hbm, lb.at[slot, pl.ds(wl[0], 2)], local_sem.at[0])
    own_l.start()
    own_v = pltpu.make_async_copy(v_hbm, vc, local_sem.at[2])
    pl.when(diag)(lambda: own_v.start())

    def forward_near(q):
        for e in (0, 1):
            w = 4 * yq[q] + 2 * e
            got(lb.at[near_row, pl.ds(w, 2)], lx_r.at[q, e])
            j = jnp.where(near == -1, 0, 1)
            half = lb.at[near_row, w + j]
            send(half, half, lf_s.at[q, e], lf_r.at[q, e, j], device(wrap(x - near, X), y, z, c))

    nexts = {1: (True, 3), 2: (False, 4), 3: (True, 5), 4: (False, 6), 5: (True, 7), 6: (False, 7)}
    for q in range(1, 8):
        got_ring_l(q)
        if q in nexts:
            ring_l(q, *nexts[q])
        spread_l(q)
        got_ring_r(q)
        if q in nexts:
            ring_r(q, *nexts[q])
        spread_r(q)
        forward_near(q - 1)
        if q == 4:

            @pl.when(diag)
            def _():
                cps = []
                for d in range(1, 8):
                    zs = wrap(z + d, Z)
                    got(vt.at[zs], vr.at[zs])
                    cp = pltpu.make_async_remote_copy(
                        src_ref=vt.at[zs], dst_ref=vc, send_sem=vfs.at[d], recv_sem=vfr.at[0],
                        device_id=device(x, zs, z, c), device_id_type=MESH,
                    )
                    cp.start()
                    cps.append(cp)
                for cp in cps:
                    cp.wait_send()

    forward_near(7)
    own_l.wait()

    own_r = pltpu.make_async_copy(rz.at[0], rb.at[pl.ds(w_own, 2)], local_sem.at[1])
    own_r.wait()
    for d, o in enumerate(OFFS):
        ys = wrap(y + o, Y)
        ref = rb.at[pl.ds(4 * ys + 2 * c, 2)]
        if d:
            got(ref, ra_r.at[ys])
        send(ref, ref, rd_s.at[d], rd_r.at[ys], device(x, y, z, other))

    @pl.when(diag)
    def _():
        own_v.wait()

    got(vc, vfr.at[0], when=jnp.logical_not(diag))

    rows = lax.broadcasted_iota(jnp.int32, (BLK, BLK), 0)
    cols = lax.broadcasted_iota(jnp.int32, (BLK, BLK), 1)
    col_size = size_ref[4 * y + x]
    masks = [
        jnp.logical_and(rows < size_ref[4 * z + 2 * c + k], cols < col_size) for k in (0, 1)
    ]
    v = [
        jnp.where(masks[k], vc[pl.ds(BLK * k, BLK)].astype(jnp.float32), 0.0) for k in (0, 1)
    ]

    for q in range(8):
        got(lb.at[same_row, pl.ds(4 * yq[q] + 2 * other, 2)], ld_r.at[q], when=own)
        for e in (0, 1):
            for j in (0, 1):
                got(
                    lb.at[same_row, 4 * yq[q] + 2 * e + j], lf_r.at[q, e, j],
                    when=jnp.logical_not(own),
                )
    for d in range(8):
        ys = wrap(y + d, Y)
        got(rb.at[pl.ds(4 * ys + 2 * other, 2)], rd_r.at[ys])

    def apply(blocks):
        def left(i, carry):
            for k in (0, 1):
                a = lb[k, pl.ds(4 * i, 4)].reshape(4 * BLK, BLK)
                p = jnp.dot(a, blocks[k], preferred_element_type=jnp.float32)
                im[pl.ds(4 * i, 4), pl.ds(BLK * k, BLK)] = p.astype(jnp.bfloat16).reshape(4, BLK, BLK)
            return carry

        lax.fori_loop(0, 8, left, 0)

        def right(i, acc):
            a = jnp.concatenate([im[2 * i], im[2 * i + 1]], axis=1)
            b = jnp.concatenate([rb[2 * i], rb[2 * i + 1]], axis=1)
            return acc + lax.dot_general(
                a, b, (((1,), (1,)), ((), ())), preferred_element_type=jnp.float32
            )

        return lax.fori_loop(0, 16, right, jnp.zeros((2 * BLK, BLK), jnp.float32))

    total = apply([b.astype(jnp.bfloat16) for b in v])
    first = [jnp.where(masks[k], total[BLK * k : BLK * (k + 1)], 0.0) for k in (0, 1)]
    first_b = [f.astype(jnp.bfloat16).astype(jnp.float32) for f in first]

    def fold(a):
        return jnp.sum(a.reshape(BLK // 8, 8, BLK), axis=0)

    num = fold(v[0] * first_b[0]) + fold(v[1] * first_b[1])
    den = fold(v[0] * v[0]) + fold(v[1] * v[1])
    part[0, 0] = num
    part[0, 1] = den

    def swap(n, buf, devs):
        for i, to in enumerate(devs):
            send(part.at[n], buf.at[i], ts.at[8 * n + i], tr.at[8 * n + i], to)

    def add(n, buf, count):
        acc = part[n]
        for i in range(count):
            got(buf.at[i], tr.at[8 * n + i])
            acc = acc + buf[i]
        part[n + 1] = acc

    swap(0, core_in, [device(x, y, z, other)])

    num0, den0 = jnp.sum(num), jnp.sum(den)
    theta0 = jnp.where(den0 > 0.0, num0 / jnp.where(den0 > 0.0, den0, 1.0), 0.0)
    for k in (0, 1):
        s1[pl.ds(BLK * k, BLK)] = first[k]
    s1[pl.ds(2 * BLK, 8)] = jnp.full((8, BLK), theta0, jnp.float32)
    home = device(x, z, y, c)
    send(s1, s1h, hs.at[0], hr.at[0], home, when=jnp.logical_not(diag))
    home_s1 = pltpu.make_async_copy(s1, s1h, local_sem.at[3])
    pl.when(diag)(lambda: home_s1.start())

    add(0, core_in, 1)
    swap(1, x_in, [device(wrap(x + d, X), y, z, c) for d in (1, 2, 3)])

    corr = [(first_b[k] - theta0 * v[k]).astype(jnp.bfloat16) for k in (0, 1)]
    total2 = apply(corr)
    for k in (0, 1):
        g[pl.ds(BLK * k, BLK)] = jnp.where(masks[k], total2[BLK * k : BLK * (k + 1)], 0.0)
    send(g, gh, hs.at[1], hr.at[1], home, when=jnp.logical_not(diag))
    home_g = pltpu.make_async_copy(g, gh, local_sem.at[4])
    pl.when(diag)(lambda: home_g.start())

    add(1, x_in, 3)
    swap(2, y_in, [device(x, wrap(y + d, Y), z, c) for d in range(1, 8)])
    add(2, y_in, 7)
    swap(3, z_in, [device(x, y, wrap(z + d, Z), c) for d in range(1, 8)])

    got(s1h, hr.at[0], when=jnp.logical_not(diag))
    got(gh, hr.at[1], when=jnp.logical_not(diag))

    @pl.when(diag)
    def _():
        home_s1.wait()
        home_g.wait()

    out1[...] = s1h[pl.ds(0, 2 * BLK)].astype(jnp.bfloat16)
    add(3, z_in, 7)
    theta = jnp.sum(part[4, 0]) / jnp.sum(part[4, 1])
    shift = theta - s1h[2 * BLK, 0]
    home_col = size_ref[4 * z + x]
    for k in (0, 1):
        mask = jnp.logical_and(rows < size_ref[4 * y + 2 * c + k], cols < home_col)
        part_k = pl.ds(BLK * k, BLK)
        out2[part_k] = jnp.where(mask, gh[part_k] - shift * s1h[part_k], 0.0).astype(jnp.bfloat16)

    for cp, when in sent:
        if when is None:
            cp.wait_send()
        else:
            pl.when(when)(lambda cp=cp: cp.wait_send())


def shards(wavefunction, left_env, right_env, sector_size):
    left = left_env.reshape(2, BLK, BLK)
    right = right_env.reshape(2, BLK, BLK)
    bf, f32 = jnp.bfloat16, jnp.float32
    any_spec = pl.BlockSpec(memory_space=pl.ANY)
    vmem = pl.BlockSpec(memory_space=pltpu.VMEM)
    dma = pltpu.SemaphoreType.DMA
    out = jax.ShapeDtypeStruct((2 * BLK, BLK), bf)
    return pl.pallas_call(
        kernel,
        out_shape=(out, out),
        in_specs=[pl.BlockSpec(memory_space=pltpu.SMEM), any_spec, any_spec, any_spec],
        out_specs=(vmem, vmem),
        scratch_shapes=[
            pltpu.VMEM((3, 32, BLK, BLK), bf),
            pltpu.VMEM((Z, 2, BLK, BLK), bf),
            pltpu.VMEM((32, BLK, BLK), bf),
            pltpu.VMEM((Z, 2 * BLK, BLK), bf),
            pltpu.VMEM((2 * BLK, BLK), bf),
            pltpu.VMEM((32, 2 * BLK, BLK), bf),
            pltpu.VMEM((2 * BLK + 8, BLK), f32),
            pltpu.VMEM((2 * BLK, BLK), f32),
            pltpu.VMEM((2 * BLK + 8, BLK), f32),
            pltpu.VMEM((2 * BLK, BLK), f32),
            pltpu.VMEM((5, 2, 8, BLK), f32),
            pltpu.VMEM((1, 2, 8, BLK), f32),
            pltpu.VMEM((3, 2, 8, BLK), f32),
            pltpu.VMEM((7, 2, 8, BLK), f32),
            pltpu.VMEM((7, 2, 8, BLK), f32),
            dma((5,)),
            dma((9,)), dma((9,)), dma((8, 2)), dma((8, 2)), dma((8,)), dma((8,)), dma((8, 2)), dma((8, 2, 2)),
            dma((9,)), dma((9,)), dma((8,)), dma((8,)), dma((8,)), dma((8,)),
            dma((1,)), dma((8,)), dma((8,)), dma((1,)), dma((2,)), dma((2,)), dma((32,)), dma((32,)),
        ],
        compiler_params=pltpu.CompilerParams(
            collective_id=0, has_side_effects=True, vmem_limit_bytes=48 << 20
        ),
        name="davidson",
    )(sector_size, wavefunction, left, right)


def solution(mesh):
    return jax.shard_map(
        shards,
        mesh=mesh,
        in_specs=(
            P("terms", "sectors"),
            P("terms", "sectors", None, None),
            P("terms", "sectors", None, None),
            P(),
        ),
        out_specs=(P("terms", "sectors"), P("terms", "sectors")),
        check_vma=False,
    )
```

time: 557 us -> 89.9 us (0.16)
  blocking collectives: 284 us -> 0 us
  waiting for transfers between devices: 197 us -> 0 us
  Pallas kernels: 0 us -> 84.6 us
  local copies, waits for them, and re-layouts: 47.9 us -> 4.43 us
  between operations: 15.2 us -> 0.65 us
  other arithmetic: 6.33 us -> 0 us
    all_to_all x4 -> x0, blocking collectives: 188 us -> none  [the longest x2 110 us: apply_ham(): lax.all_to_all(image, 'sectors', split_axis=2, concat_axis=1, tiled=True)]
    reduce_scatter x2 -> x0, waiting for transfers between devices: 112 us -> none  [apply_ham(): lax.psum_scatter(partial_sum, 'terms', scatter_dimension=0, tiled=True)]
    psum x1 -> x0, blocking collectives: 96.6 us -> none  [shards(): lax.psum((jnp.sum(start_wide * first_wide), jnp.sum(start_wide * start_wi...]
    all_gather x2 -> x0, waiting for transfers between devices: 85.1 us -> none  [apply_ham(): column_part = lax.all_gather(masked, 'terms', axis=0, tiled=True)]
    pallas_call x0 -> x1, Pallas kernels: none -> 84.6 us  [shards(): pl.pallas_call(kernel, out_shape=(out, out), in_specs=[pl.BlockSpec(memor...]
    reshape x2 -> x0, local copies, waits for them, and re-layouts: 35.6 us -> none  [apply_ham(): image.astype(jnp.bfloat16).reshape(left_env.shape[0], col_count, full_dim)]
    all_to_all x4 -> x0, local copies, waits for them, and re-layouts: 12.1 us -> none  [the longest x2 9.81 us: apply_ham(): lax.all_to_all(image, 'sectors', split_axis=2, concat_axis=1, tiled=True)]
  transfers between devices with their start and end apart: 4 -> 0, of which waited for: 4 -> 0; matrix products, arithmetic and copies ran while one was open for 0% -> 0% of each run, Pallas kernels for 0% -> 0%
where the time goes in v1:
time: 89.9 us; the launch traced here: 89.6 us
  Pallas kernels  84.6 us (94%)
  local copies, waits for them, and re-layouts  4.43 us (5%)
    pallas_call x1, Pallas kernels, shards(): pl.pallas_call(kernel, out_shape=(out, out), in_specs=[pl.BlockSpec(memor...  84.6 us
    unnamed x10, local copies, waits for them, and re-layouts  4.43 us

profile of v1, /device:TPU:6, one launch (start us, length us, event | category | flops | bytes accessed | tf_op | source)
XLA Modules:
  0.0 89.6 jit_solution(1207631573797474355)
XLA Ops:
  0.6 0.0 copy-start.3
  0.6 0.6 copy-done.3
  1.3 0.0 copy-start
  1.3 0.8 copy-done
  2.1 0.0 copy-start.1
  2.1 0.8 copy-done.1
  3.0 0.0 copy-start.2
  3.0 0.8 copy-done.2
  3.8 84.6 %davidson.1 = (bf16[256,128]{1,0:T(8,128)(2,1)S(1)}, bf16[256,128]{1,0:T(8,128)(2,1)S(1)}) custom-call(s32[32]{0:T(128)S(1)} %copy-done.3, bf16[256,128]{1,0:T(8,128)(2,1)S(1)} %copy-done, bf16[2,128,128]{2,1,0:T(8,128)(2,1)S(1)} %bitcast.2, bf16[2,128,128]{2,1,0:T(8,128)(2,1)S(1)} %bitcast.3), custom_call_target="tpu_custom_call" | custom-call | tf_op jit(solution)/shard_map/davidson/pallas_call | solution.py:327
  88.4 0.6 copy.8
  89.0 0.6 copy.9
Async XLA Ops:
  0.6 0.7 copy-start.3
  1.3 0.8 copy-start
  2.1 0.8 copy-start.1
  3.0 0.8 copy-start.2

commit v2 on v0

v2 whole, which is shorter than its diff:
```python
import jax
import jax.numpy as jnp
from jax import lax
from jax.experimental import pallas as pl
from jax.experimental.pallas import tpu as pltpu
from jax.sharding import PartitionSpec as P

MESH = pl.DeviceIdType.MESH
BLK = 128
X, Y, Z = 4, 8, 8
OFFS = (0, -1, 1, -2, 2, -3, 3, 4)


def wrap(value, n):
    return lax.rem(value + 2 * n, n)


def device(x, y, z, c):
    return {"terms": 2 * y + c, "sectors": 4 * z + x}


def kernel(
    size_hbm, v_hbm, l_hbm, r_hbm, out1, out2,
    sizes, rb, ls, vc, im, s1, g, s1h, gh, part, x_in, y_in, z_in,
    local, ry_s, ry_r, rx_s, rx_r, rd_s, rd_r, rf_s, rf_r,
    lt_s, lt_r, lz_s, lz_r, ld_s, ld_r, v_s, v_r, h_s, h_r, t_s, t_r,
):
    t, s = lax.axis_index("terms"), lax.axis_index("sectors")
    y, c = t // 2, lax.rem(t, 2)
    z, x = s // 4, lax.rem(s, 4)
    other = 1 - c
    ct = x // 2
    own = c == ct
    odd = lax.rem(x, 2)
    slot = jnp.where(own, odd, 2)
    outer = jnp.logical_or(x == 0, x == 3)
    near = jnp.where(outer != (c == 1), 1, -1)
    diag = y == z
    off_diag = jnp.logical_not(diag)
    not_own = jnp.logical_not(own)

    barrier = pltpu.get_barrier_semaphore()
    peers = [device(x, y, z, other)]
    for d in (1, 2, 3):
        for e in (0, 1):
            peers.append(device(wrap(x + d, X), y, z, e))
    for d in range(1, 8):
        peers.append(device(x, wrap(y + d, Y), z, c))
        peers.append(device(x, y, wrap(z + d, Z), c))
    across = device(x, z, y, c)

    def hello(to):
        pl.semaphore_signal(barrier, inc=1, device_id=to, device_id_type=MESH)

    pl.when(off_diag)(lambda: hello(across))
    for p in peers:
        hello(p)

    def mine(ref):
        return lambda w: ref.at[pl.ds(w, 2)]

    get_sizes = pltpu.make_async_copy(size_hbm, sizes, local.at[0])
    get_sizes.start()
    own_r = pltpu.make_async_copy(r_hbm, rb.at[slot, pl.ds(4 * y + 2 * c, 2)], local.at[1])
    own_r.start()
    own_l = pltpu.make_async_copy(l_hbm, ls.at[pl.ds(4 * z + 2 * c, 2)], local.at[2])
    pl.when(diag)(lambda: own_l.start())
    own_v = pltpu.make_async_copy(v_hbm.at[pl.ds(BLK * odd, BLK)], vc.at[odd], local.at[3])
    pl.when(own)(lambda: own_v.start())

    pl.semaphore_wait(barrier, len(peers) + jnp.where(diag, 0, 1))

    sent = []

    def send(src, dst, ssem, rsem, to, when=None):
        cp = pltpu.make_async_remote_copy(
            src_ref=src, dst_ref=dst, send_sem=ssem, recv_sem=rsem, device_id=to, device_id_type=MESH
        )
        if when is None:
            cp.start()
        else:
            pl.when(when)(lambda: cp.start())
        sent.append((cp, when))

    def got(dst, rsem, when=None):
        cp = pltpu.make_async_remote_copy(
            src_ref=dst, dst_ref=dst, send_sem=rsem, recv_sem=rsem,
            device_id=device(x, y, z, other), device_id_type=MESH,
        )
        if when is None:
            cp.wait_recv()
        else:
            pl.when(when)(lambda: cp.wait_recv())

    yq = [wrap(y + o, Y) for o in OFFS]
    wr = [4 * v + 2 * c for v in yq]

    def piece_r(q):
        return r_hbm if q == 0 else rb.at[slot, pl.ds(wr[q], 2)]

    def pass_r(q, step, to_q):
        to = device(x, wrap(y + step, Y), z, c)
        if to_q < 7:
            send(piece_r(q), rb.at[slot, pl.ds(wr[q], 2)], ry_s.at[to_q], ry_r.at[to_q], to)
        else:
            i = 0 if step > 0 else 1
            half = rb.at[slot, wr[q] + i]
            send(half, half, ry_s.at[7 + i], ry_r.at[7 + i], to)

    def got_r(q):
        if q < 7:
            got(rb.at[slot, pl.ds(wr[q], 2)], ry_r.at[q])
        else:
            for i in (0, 1):
                got(rb.at[slot, wr[q] + i], ry_r.at[7 + i])

    def spread_r(q):
        dst = rb.at[odd, pl.ds(wr[q], 2)]
        for e, d in enumerate((1, -1)):
            send(piece_r(q), dst, rx_s.at[q, e], rx_r.at[q, c], device(wrap(x + d, X), y, z, ct))
        send(piece_r(q), dst, rd_s.at[q], rd_r.at[q], device(x, y, z, other), when=not_own)

    def beyond(q):
        for e in (0, 1):
            w = 4 * yq[q] + 2 * e
            got(rb.at[1 - odd, pl.ds(w, 2)], rx_r.at[q, e])
            j = jnp.where(near == -1, 0, 1)
            half = rb.at[1 - odd, w + j]
            send(half, half, rf_s.at[q, e], rf_r.at[q, e, j], device(wrap(x - near, X), y, z, c))

    def got_far(q):
        got(rb.at[odd, pl.ds(4 * yq[q] + 2 * other, 2)], rd_r.at[q], when=own)
        for e in (0, 1):
            for j in (0, 1):
                got(rb.at[odd, 4 * yq[q] + 2 * e + j], rf_r.at[q, e, j], when=not_own)

    zq = [wrap(z + o, Z) for o in OFFS]
    wz = [4 * v + 2 * c for v in zq]

    def pass_l(q, step, to_q):
        to = device(x, y, wrap(z + step, Z), c)
        if to_q < 7:
            ref = ls.at[pl.ds(wz[q], 2)]
            send(ref, ref, lz_s.at[to_q], lz_r.at[to_q], to)
        else:
            i = 0 if step > 0 else 1
            half = ls.at[wz[q] + i]
            send(half, half, lz_s.at[7 + i], lz_r.at[7 + i], to)

    def got_l(q):
        if q == 0:
            got(ls.at[pl.ds(wz[0], 2)], lt_r.at[0], when=off_diag)
            pl.when(diag)(lambda: own_l.wait())
        elif q < 7:
            got(ls.at[pl.ds(wz[q], 2)], lz_r.at[q])
        else:
            for i in (0, 1):
                got(ls.at[wz[q] + i], lz_r.at[7 + i])
        ref = ls.at[pl.ds(wz[q], 2)]
        send(ref, ref, ld_s.at[q], ld_r.at[q], device(x, y, z, other))

    def got_l_other(q):
        got(ls.at[pl.ds(4 * zq[q] + 2 * other, 2)], ld_r.at[q])

    relay = {1: (2, 5), 2: (-2, 6), 3: (2, 7), 4: (-2, 7)}
    first_steps = ((1, 1), (-1, 2), (2, 3), (-2, 4))

    send(l_hbm, ls.at[pl.ds(4 * y + 2 * c, 2)], lt_s.at[0], lt_r.at[0], across, when=off_diag)
    for step, to_q in first_steps:
        pass_r(0, step, to_q)
    spread_r(0)
    for k in (0, 1):
        keep = jnp.logical_and(own, odd == k)
        send(
            v_hbm.at[pl.ds(BLK * k, BLK)], vc.at[odd], v_s.at[k], v_r.at[odd],
            device(2 * c + k, y, z, ct), when=jnp.logical_not(keep),
        )

    def do_r(q):
        got_r(q)
        if q in relay:
            pass_r(q, *relay[q])
        spread_r(q)

    def do_l(q):
        got_l(q)
        if q in relay:
            pass_l(q, *relay[q])

    do_r(1)
    do_r(2)
    beyond(0)
    do_r(3)
    do_r(4)
    beyond(1)
    got_l(0)
    for step, to_q in first_steps:
        pass_l(0, step, to_q)
    beyond(2)
    do_r(5)
    do_r(6)
    do_r(7)
    beyond(3)
    beyond(4)
    do_l(1)
    do_l(2)
    beyond(5)
    do_l(3)
    do_l(4)
    beyond(6)
    beyond(7)

    get_sizes.wait()
    own_r.wait()
    pl.when(own)(lambda: own_v.wait())
    for k in (0, 1):
        keep = jnp.logical_and(own, odd == k)
        got(vc.at[k], v_r.at[k], when=jnp.logical_not(keep))
    rows = lax.broadcasted_iota(jnp.int32, (BLK, BLK), 0)
    cols = lax.broadcasted_iota(jnp.int32, (BLK, BLK), 1)
    row_live = rows < sizes[4 * y + x]
    masks = [jnp.logical_and(row_live, cols < sizes[4 * z + 2 * c + k]) for k in (0, 1)]
    v = [jnp.where(masks[k], vc[k].astype(jnp.float32), 0.0) for k in (0, 1)]

    def left(group, both):
        a = ls[pl.ds(4 * group, 4)].reshape(4 * BLK, BLK)
        p = jnp.dot(a, both, preferred_element_type=jnp.float32)
        im[pl.ds(4 * group, 4)] = p.astype(jnp.bfloat16).reshape(4, BLK, 2 * BLK)

    def right(group, acc):
        new = []
        for k in (0, 1):
            a = jnp.concatenate(
                [im[4 * group + i, :, pl.ds(BLK * k, BLK)] for i in range(4)], axis=1
            )
            b = jnp.concatenate([rb[k, 4 * group + i] for i in range(4)], axis=1)
            p = lax.dot_general(a, b, (((1,), (1,)), ((), ())), preferred_element_type=jnp.float32)
            new.append(acc[k] + p)
        return tuple(new)

    zero = (jnp.zeros((BLK, BLK), jnp.float32),) * 2
    both = jnp.concatenate([b.astype(jnp.bfloat16) for b in v], axis=1)
    for q in range(8):
        if q >= 5:
            got_l(q)
        got_l_other(q)
        left(zq[q], both)
    total = zero
    for q in range(8):
        got_far(q)
        total = right(yq[q], total)

    first = [jnp.where(masks[k], total[k], 0.0) for k in (0, 1)]
    first_b = [f.astype(jnp.bfloat16).astype(jnp.float32) for f in first]

    def fold(a):
        return jnp.sum(a.reshape(BLK // 8, 8, BLK), axis=0)

    num = fold(v[0] * first_b[0]) + fold(v[1] * first_b[1])
    den = fold(v[0] * v[0]) + fold(v[1] * v[1])
    part[0, 0] = num
    part[0, 1] = den

    def swap(n, buf, devs):
        for i, to in enumerate(devs):
            send(part.at[n], buf.at[i], t_s.at[8 * n + i], t_r.at[8 * n + i], to)

    def add(n, buf):
        acc = part[n]
        for i in range(7):
            got(buf.at[i], t_r.at[8 * n + i])
            acc = acc + buf[i]
        part[n + 1] = acc

    swap(0, x_in, [device(wrap(x + d // 2, X), y, z, wrap(c + d, 2)) for d in range(1, 8)])

    num0, den0 = jnp.sum(num), jnp.sum(den)
    theta0 = jnp.where(den0 > 0.0, num0 / jnp.where(den0 > 0.0, den0, 1.0), 0.0)

    def go_home(k, src, dst, n):
        keep = jnp.logical_and(own, odd == k)
        send(
            src.at[k], dst.at[odd], h_s.at[n, k], h_r.at[n, odd],
            device(2 * c + k, y, z, ct), when=jnp.logical_not(keep),
        )
        cp = pltpu.make_async_copy(src.at[k], dst.at[odd], local.at[4 + n])
        pl.when(keep)(lambda: cp.start())

    def got_home(dst, n):
        for k in (0, 1):
            keep = jnp.logical_and(own, odd == k)
            got(dst.at[k], h_r.at[n, k], when=jnp.logical_not(keep))
            cp = pltpu.make_async_copy(dst.at[k], dst.at[k], local.at[4 + n])
            pl.when(keep)(lambda: cp.wait())

    for k in (0, 1):
        s1[k, pl.ds(0, BLK)] = first[k]
        s1[k, pl.ds(BLK, 8)] = jnp.full((8, BLK), theta0, jnp.float32)
        go_home(k, s1, s1h, 0)

    corr = jnp.concatenate([(first_b[k] - theta0 * v[k]).astype(jnp.bfloat16) for k in (0, 1)], axis=1)

    def left_loop(i, carry):
        left(i, corr)
        return carry

    lax.fori_loop(0, 8, left_loop, 0)
    add(0, x_in)
    swap(1, y_in, [device(x, wrap(y + d, Y), z, c) for d in range(1, 8)])
    total2 = lax.fori_loop(0, 8, right, zero)
    for k in (0, 1):
        g[k] = jnp.where(masks[k], total2[k], 0.0)
        go_home(k, g, gh, 1)
    add(1, y_in)
    swap(2, z_in, [device(x, y, wrap(z + d, Z), c) for d in range(1, 8)])

    got_home(s1h, 0)
    got_home(gh, 1)
    for k in (0, 1):
        out1[pl.ds(BLK * k, BLK)] = s1h[k, pl.ds(0, BLK)].astype(jnp.bfloat16)
    for cp, when in sent:
        if when is None:
            cp.wait_send()
        else:
            pl.when(when)(lambda cp=cp: cp.wait_send())
    add(2, z_in)
    theta = jnp.sum(part[3, 0]) / jnp.sum(part[3, 1])
    home_live = cols < sizes[4 * z + x]
    for k in (0, 1):
        mask = jnp.logical_and(rows < sizes[4 * y + 2 * c + k], home_live)
        shift = theta - s1h[k, BLK, 0]
        new = gh[k] - shift * s1h[k, pl.ds(0, BLK)]
        out2[pl.ds(BLK * k, BLK)] = jnp.where(mask, new, 0.0).astype(jnp.bfloat16)


def shards(wavefunction, left_env, right_env, sector_size):
    left = left_env.reshape(2, BLK, BLK)
    right = right_env.reshape(2, BLK, BLK)
    bf, f32 = jnp.bfloat16, jnp.float32
    hbm = pl.BlockSpec(memory_space=pltpu.MemorySpace.HBM)
    vmem = pl.BlockSpec(memory_space=pltpu.VMEM)
    dma = pltpu.SemaphoreType.DMA
    out = jax.ShapeDtypeStruct((2 * BLK, BLK), bf)
    return pl.pallas_call(
        kernel,
        out_shape=(out, out),
        in_specs=[hbm, hbm, hbm, hbm],
        out_specs=(vmem, vmem),
        scratch_shapes=[
            pltpu.SMEM((32,), jnp.int32),
            pltpu.VMEM((3, 32, BLK, BLK), bf),
            pltpu.VMEM((32, BLK, BLK), bf),
            pltpu.VMEM((2, BLK, BLK), bf),
            pltpu.VMEM((32, BLK, 2 * BLK), bf),
            pltpu.VMEM((2, BLK + 8, BLK), f32),
            pltpu.VMEM((2, BLK, BLK), f32),
            pltpu.VMEM((2, BLK + 8, BLK), f32),
            pltpu.VMEM((2, BLK, BLK), f32),
            pltpu.VMEM((4, 2, 8, BLK), f32),
            pltpu.VMEM((7, 2, 8, BLK), f32),
            pltpu.VMEM((7, 2, 8, BLK), f32),
            pltpu.VMEM((7, 2, 8, BLK), f32),
            dma((6,)),
            dma((9,)), dma((9,)), dma((8, 2)), dma((8, 2)), dma((8,)), dma((8,)), dma((8, 2)), dma((8, 2, 2)),
            dma((1,)), dma((1,)), dma((9,)), dma((9,)), dma((8,)), dma((8,)),
            dma((2,)), dma((2,)), dma((2, 2)), dma((2, 2)), dma((24,)), dma((24,)),
        ],
        compiler_params=pltpu.CompilerParams(
            collective_id=0, has_side_effects=True, vmem_limit_bytes=48 << 20
        ),
        name="davidson",
    )(sector_size, wavefunction, left, right)


def solution(mesh):
    return jax.shard_map(
        shards,
        mesh=mesh,
        in_specs=(
            P("terms", "sectors"),
            P("terms", "sectors", None, None),
            P("terms", "sectors", None, None),
            P(),
        ),
        out_specs=(P("terms", "sectors"), P("terms", "sectors")),
        check_vma=False,
    )
```

time: 557 us -> 63.3 us (0.11)
  blocking collectives: 284 us -> 0 us
  waiting for transfers between devices: 197 us -> 0 us
  Pallas kernels: 0 us -> 57.3 us
  local copies, waits for them, and re-layouts: 47.9 us -> 4.43 us
  between operations: 15.2 us -> 0.65 us
  other arithmetic: 6.33 us -> 0 us
    all_to_all x4 -> x0, blocking collectives: 188 us -> none  [the longest x2 110 us: apply_ham(): lax.all_to_all(image, 'sectors', split_axis=2, concat_axis=1, tiled=True)]
    reduce_scatter x2 -> x0, waiting for transfers between devices: 112 us -> none  [apply_ham(): lax.psum_scatter(partial_sum, 'terms', scatter_dimension=0, tiled=True)]
    psum x1 -> x0, blocking collectives: 96.6 us -> none  [shards(): lax.psum((jnp.sum(start_wide * first_wide), jnp.sum(start_wide * start_wi...]
    all_gather x2 -> x0, waiting for transfers between devices: 85.1 us -> none  [apply_ham(): column_part = lax.all_gather(masked, 'terms', axis=0, tiled=True)]
    pallas_call x0 -> x1, Pallas kernels: none -> 57.3 us  [shards(): pl.pallas_call(kernel, out_shape=(out, out), in_specs=[hbm, hbm, hbm, hbm...]
    reshape x2 -> x0, local copies, waits for them, and re-layouts: 35.6 us -> none  [apply_ham(): image.astype(jnp.bfloat16).reshape(left_env.shape[0], col_count, full_dim)]
    all_to_all x4 -> x0, local copies, waits for them, and re-layouts: 12.1 us -> none  [the longest x2 9.81 us: apply_ham(): lax.all_to_all(image, 'sectors', split_axis=2, concat_axis=1, tiled=True)]
  transfers between devices with their start and end apart: 4 -> 0, of which waited for: 4 -> 0; matrix products, arithmetic and copies ran while one was open for 0% -> 0% of each run, Pallas kernels for 0% -> 0%
where the time goes in v2:
time: 63.3 us; the launch traced here: 62.3 us
  Pallas kernels  57.3 us (91%)
  local copies, waits for them, and re-layouts  4.43 us (7%)
  between operations  0.65 us (1%)
    pallas_call x1, Pallas kernels, shards(): pl.pallas_call(kernel, out_shape=(out, out), in_specs=[hbm, hbm, hbm, hbm...  57.3 us
    unnamed x10, local copies, waits for them, and re-layouts  4.43 us

profile of v2, /device:TPU:6, one launch (start us, length us, event | category | flops | bytes accessed | tf_op | source)
XLA Modules:
  0.0 62.3 jit_solution(3359989372024176572)
XLA Ops:
  0.6 0.0 copy-start.3
  0.6 0.6 %copy-done.3 = s32[32]{0:T(128)S(1)} copy-done((s32[32]{0:T(128)S(1)}, s32[32]{0:T(128)}, u32[]{:S(2)}) %copy-start.3) | copy-done | bytes 152
  1.3 0.0 copy-start
  1.3 0.8 %copy-done = bf16[256,128]{1,0:T(8,128)(2,1)S(1)} copy-done((bf16[256,128]{1,0:T(8,128)(2,1)S(1)}, bf16[256,128]{1,0:T(8,128)(2,1)}, u32[]{:S(2)}) %copy-start) | copy-done | bytes 65560
  2.1 0.0 copy-start.1
  2.1 0.8 %copy-done.1 = bf16[2,1,128,128]{3,2,1,0:T(8,128)(2,1)S(1)} copy-done((bf16[2,1,128,128]{3,2,1,0:T(8,128)(2,1)S(1)}, bf16[2,1,128,128]{3,2,1,0:T(8,128)(2,1)}, u32[]{:S(2)}) %copy-start.1) | copy-done | bytes 65560
  3.0 0.0 copy-start.2
  3.0 0.8 %copy-done.2 = bf16[2,1,128,128]{3,2,1,0:T(8,128)(2,1)S(1)} copy-done((bf16[2,1,128,128]{3,2,1,0:T(8,128)(2,1)S(1)}, bf16[2,1,128,128]{3,2,1,0:T(8,128)(2,1)}, u32[]{:S(2)}) %copy-start.2) | copy-done | bytes 65560
  3.8 57.3 %davidson.1 = (bf16[256,128]{1,0:T(8,128)(2,1)S(1)}, bf16[256,128]{1,0:T(8,128)(2,1)S(1)}) custom-call(s32[32]{0:T(128)S(1)} %copy-done.3, bf16[256,128]{1,0:T(8,128)(2,1)S(1)} %copy-done, bf16[2,128,128]{2,1,0:T(8,128)(2,1)S(1)} %bitcast.2, bf16[2,128,128]{2,1,0:T(8,128)(2,1)S(1)} %bitcast.3), custom_call_target="tpu_custom_call" | custom-call | tf_op jit(solution)/shard_map/davidson/pallas_call | solution.py:344
  61.1 0.6 %copy.8 = bf16[256,128]{1,0:T(8,128)(2,1)} copy(bf16[256,128]{1,0:T(8,128)(2,1)S(1)} %get-tuple-element.4) | data formatting | bytes 131072
  61.7 0.6 %copy.9 = bf16[256,128]{1,0:T(8,128)(2,1)} copy(bf16[256,128]{1,0:T(8,128)(2,1)S(1)} %get-tuple-element.5) | data formatting | bytes 131072
Async XLA Ops:
  0.6 0.7 %copy-start.3 = (s32[32]{0:T(128)S(1)}, s32[32]{0:T(128)}, u32[]{:S(2)}) copy-start(s32[32]{0:T(128)} %size_hbm.1) | copy-start | bytes 388
  1.3 0.8 %copy-start = (bf16[256,128]{1,0:T(8,128)(2,1)S(1)}, bf16[256,128]{1,0:T(8,128)(2,1)}, u32[]{:S(2)}) copy-start(bf16[256,128]{1,0:T(8,128)(2,1)} %v_hbm.1) | copy-start | bytes 196612
  2.1 0.8 %copy-start.1 = (bf16[2,1,128,128]{3,2,1,0:T(8,128)(2,1)S(1)}, bf16[2,1,128,128]{3,2,1,0:T(8,128)(2,1)}, u32[]{:S(2)}) copy-start(bf16[2,1,128,128]{3,2,1,0:T(8,128)(2,1)} %param.5) | copy-start | bytes 196612
  3.0 0.8 %copy-start.2 = (bf16[2,1,128,128]{3,2,1,0:T(8,128)(2,1)S(1)}, bf16[2,1,128,128]{3,2,1,0:T(8,128)(2,1)}, u32[]{:S(2)}) copy-start(bf16[2,1,128,128]{3,2,1,0:T(8,128)(2,1)} %param.6) | copy-start | bytes 196612

commit v3 on v2

v3 whole, which is shorter than its diff:
```python
import jax
import jax.numpy as jnp
from jax import lax
from jax.experimental import pallas as pl
from jax.experimental.pallas import tpu as pltpu
from jax.sharding import PartitionSpec as P

MESH = pl.DeviceIdType.MESH
BLK = 128
X, Y, Z = 4, 8, 8
R_RELAY = {0: ((1, 1), (-1, 2)), 1: ((1, 3),), 2: ((-1, 4),), 3: ((1, 5),), 4: ((-1, 6),), 5: ((1, 7),), 6: ((-1, 7),)}
L_RELAY = {0: ((1, 1), (-1, 2), (2, 3), (-2, 4)), 1: ((2, 5),), 2: ((-2, 6),), 3: ((2, 7),), 4: ((-2, 7),)}
OFFS = (0, -1, 1, -2, 2, -3, 3, 4)


def wrap(value, n):
    return lax.rem(value + 2 * n, n)


def device(x, y, z, c):
    return {"terms": 2 * y + c, "sectors": 4 * z + x}


def kernel(
    size_hbm, v_hbm, l_hbm, r_hbm, out1, out2,
    sizes, v_own, l_own, rb, ls, vc, im, s1, g, s1h, gh, part, x_in, y_in, z_in,
    local, ry_s, ry_r, rx_s, rx_r, rd_s, rd_r,
    la_s, la_r, lz_s, lz_r, lx_s, lx_r, ld_s, ld_r, v_s, v_r, h_s, h_r, t_s, t_r,
):
    t, s = lax.axis_index("terms"), lax.axis_index("sectors")
    y, c = t // 2, lax.rem(t, 2)
    z, x = s // 4, lax.rem(s, 4)
    other = 1 - c
    xl, xr = x + 1 - 2 * lax.rem(x, 2), 3 - x
    lcore = lax.rem(x, 2)
    own_l = c == lcore
    not_own_l = jnp.logical_not(own_l)
    lslot = jnp.where(own_l, 0, 1)
    hcore = x // 2
    own_v = c == hcore
    diag = y == z
    off_diag = jnp.logical_not(diag)

    barrier = pltpu.get_barrier_semaphore()
    peers = [device(x, y, z, other)]
    for d in (1, 2, 3):
        for e in (0, 1):
            peers.append(device(wrap(x + d, X), y, z, e))
    for d in range(1, 8):
        peers.append(device(x, wrap(y + d, Y), z, c))
        peers.append(device(x, y, wrap(z + d, Z), c))
    across = device(x, z, y, c)

    def hello(to):
        pl.semaphore_signal(barrier, inc=1, device_id=to, device_id_type=MESH)

    pl.when(off_diag)(lambda: hello(across))
    for p in reversed(peers):
        hello(p)

    get_sizes = pltpu.make_async_copy(size_hbm, sizes, local.at[0])
    get_sizes.start()
    own_r = pltpu.make_async_copy(r_hbm, rb.at[0, pl.ds(4 * y + 2 * c, 2)], local.at[1])
    own_r.start()
    get_l = pltpu.make_async_copy(l_hbm, l_own, local.at[2])
    get_l.start()
    get_v = pltpu.make_async_copy(v_hbm, v_own, local.at[3])
    get_v.start()
    get_sizes.wait()
    own_r.wait()
    get_l.wait()
    get_v.wait()
    pl.semaphore_wait(barrier, len(peers) + jnp.where(diag, 0, 1))

    sent = []

    def send(src, dst, ssem, rsem, to, when=None):
        cp = pltpu.make_async_remote_copy(
            src_ref=src, dst_ref=dst, send_sem=ssem, recv_sem=rsem, device_id=to, device_id_type=MESH
        )
        if when is None:
            cp.start()
        else:
            pl.when(when)(lambda: cp.start())
        sent.append((cp, when))

    def got(dst, rsem, when=None):
        cp = pltpu.make_async_remote_copy(
            src_ref=dst, dst_ref=dst, send_sem=rsem, recv_sem=rsem,
            device_id=device(x, y, z, other), device_id_type=MESH,
        )
        if when is None:
            cp.wait_recv()
        else:
            pl.when(when)(lambda: cp.wait_recv())

    yq = [wrap(y + o, Y) for o in OFFS]
    wr = [4 * v + 2 * c for v in yq]
    wo = [4 * v + 2 * other for v in yq]
    sibling = device(x, y, z, other)

    def pass_r(q, step, to_q):
        to = device(x, wrap(y + step, Y), z, c)
        if to_q < 7:
            ref = rb.at[0, pl.ds(wr[q], 2)]
            send(ref, ref, ry_s.at[to_q], ry_r.at[to_q], to)
        else:
            i = 0 if step > 0 else 1
            half = rb.at[0, wr[q] + i]
            send(half, half, ry_s.at[7 + i], ry_r.at[7 + i], to)

    def got_r(q):
        if q < 7:
            got(rb.at[0, pl.ds(wr[q], 2)], ry_r.at[q])
        else:
            for i in (0, 1):
                got(rb.at[0, wr[q] + i], ry_r.at[7 + i])

    def spread_r(q):
        ref = rb.at[0, pl.ds(wr[q], 2)]
        send(ref, rb.at[1, pl.ds(wr[q], 2)], rx_s.at[q], rx_r.at[q], device(xr, y, z, c))
        send(ref, ref, rd_s.at[0, q], rd_r.at[0, q], sibling)

    def beyond(q):
        ref = rb.at[1, pl.ds(wr[q], 2)]
        got(ref, rx_r.at[q])
        send(ref, ref, rd_s.at[1, q], rd_r.at[1, q], sibling)

    def got_far(q):
        for k in (0, 1):
            got(rb.at[k, pl.ds(wo[q], 2)], rd_r.at[k, q])

    zq = [wrap(z + o, Z) for o in OFFS]
    wz = [4 * v + 2 * c for v in zq]
    wzo = [4 * v + 2 * other for v in zq]

    def start_l():
        dst = ls.at[lslot, pl.ds(4 * y + 2 * c, 2)]
        send(l_own, dst, la_s.at[0], la_r.at[0], across, when=off_diag)
        cp = pltpu.make_async_copy(l_own, dst, local.at[2])
        pl.when(diag)(lambda: cp.start())

    def pass_l(q, step, to_q):
        to = device(x, y, wrap(z + step, Z), c)
        if to_q < 7:
            ref = ls.at[lslot, pl.ds(wz[q], 2)]
            send(ref, ref, lz_s.at[to_q], lz_r.at[to_q], to)
        else:
            i = 0 if step > 0 else 1
            half = ls.at[lslot, wz[q] + i]
            send(half, half, lz_s.at[7 + i], lz_r.at[7 + i], to)

    def got_l(q):
        ref = ls.at[lslot, pl.ds(wz[q], 2)]
        if q == 0:
            cp = pltpu.make_async_copy(l_own, ref, local.at[2])
            pl.when(diag)(lambda: cp.wait())
            got(ref, la_r.at[0], when=off_diag)
        elif q < 7:
            got(ref, lz_r.at[q])
        else:
            for i in (0, 1):
                got(ls.at[lslot, wz[q] + i], lz_r.at[7 + i])

    def do_l(q):
        got_l(q)
        for step, to_q in L_RELAY.get(q, ()):
            pass_l(q, step, to_q)
        ref = ls.at[lslot, pl.ds(wz[q], 2)]
        dst = ls.at[0, pl.ds(wz[q], 2)]
        send(ref, dst, lx_s.at[q], lx_r.at[q, c], device(xl, y, z, lcore))
        send(ref, dst, ld_s.at[q], ld_r.at[q], sibling, when=not_own_l)

    def got_l_other(q):
        got(ls.at[0, pl.ds(wzo[q], 2)], ld_r.at[q], when=own_l)
        for e in (0, 1):
            got(ls.at[0, pl.ds(4 * zq[q] + 2 * e, 2)], lx_r.at[q, e], when=not_own_l)

    def do_r(q):
        got_r(q)
        for step, to_q in R_RELAY.get(q, ()):
            pass_r(q, step, to_q)
        spread_r(q)

    start_l()
    for step, to_q in R_RELAY[0]:
        pass_r(0, step, to_q)
    spread_r(0)
    v_chip = jnp.where(own_v, x, xr)
    v_slot = jnp.where(own_v, 0, 1)
    for k in (0, 1):
        keep = jnp.logical_and(own_v, c == k)
        src = v_own.at[pl.ds(BLK * k, BLK)]
        send(
            src, vc.at[v_slot], v_s.at[k], v_r.at[v_slot],
            device(v_chip, y, z, k), when=jnp.logical_not(keep),
        )
        cp = pltpu.make_async_copy(src, vc.at[0], local.at[3])
        pl.when(keep)(lambda: cp.start())
    do_r(1)
    do_r(2)
    beyond(0)
    do_r(3)
    do_r(4)
    beyond(1)
    beyond(2)
    do_l(0)
    do_r(5)
    do_r(6)
    beyond(3)
    beyond(4)
    do_r(7)
    beyond(5)
    beyond(6)
    do_l(1)
    do_l(2)
    do_l(3)
    do_l(4)
    beyond(7)
    do_l(5)
    do_l(6)
    do_l(7)

    got(vc.at[0], v_r.at[0], when=jnp.logical_not(own_v))
    own_block = pltpu.make_async_copy(vc.at[0], vc.at[0], local.at[3])
    pl.when(own_v)(lambda: own_block.wait())
    got(vc.at[1], v_r.at[1])
    rows = lax.broadcasted_iota(jnp.int32, (BLK, BLK), 0)
    cols = lax.broadcasted_iota(jnp.int32, (BLK, BLK), 1)
    row_live = rows < sizes[4 * y + 2 * hcore + c]
    masks = [jnp.logical_and(row_live, cols < sizes[4 * z + n]) for n in (x, xr)]
    v = [jnp.where(masks[k], vc[k].astype(jnp.float32), 0.0) for k in (0, 1)]

    def left(group, both):
        a = ls[0, pl.ds(4 * group, 4)].reshape(4 * BLK, BLK)
        p = jnp.dot(a, both, preferred_element_type=jnp.float32)
        im[pl.ds(4 * group, 4)] = p.astype(jnp.bfloat16).reshape(4, BLK, 2 * BLK)

    def right(group, acc):
        new = []
        for k in (0, 1):
            a = jnp.concatenate(
                [im[4 * group + i, :, pl.ds(BLK * k, BLK)] for i in range(4)], axis=1
            )
            b = jnp.concatenate([rb[k, 4 * group + i] for i in range(4)], axis=1)
            p = lax.dot_general(a, b, (((1,), (1,)), ((), ())), preferred_element_type=jnp.float32)
            new.append(acc[k] + p)
        return tuple(new)

    zero = (jnp.zeros((BLK, BLK), jnp.float32),) * 2
    both = jnp.concatenate([b.astype(jnp.bfloat16) for b in v], axis=1)
    for q in range(5):
        got_l_other(q)
        left(zq[q], both)
    for q in range(8):
        got_far(q)
    total = zero
    for q in range(5):
        total = right(zq[q], total)
    for q in range(5, 8):
        got_l_other(q)
        left(zq[q], both)
        total = right(zq[q], total)

    first = [jnp.where(masks[k], total[k], 0.0) for k in (0, 1)]
    first_b = [f.astype(jnp.bfloat16).astype(jnp.float32) for f in first]

    def fold(a):
        return jnp.sum(a.reshape(BLK // 8, 8, BLK), axis=0)

    def fold_more(a):
        return a[:4] + a[4:]

    num = fold_more(fold(v[0] * first_b[0]) + fold(v[1] * first_b[1]))
    den = fold_more(fold(v[0] * v[0]) + fold(v[1] * v[1]))
    part[0] = jnp.concatenate([num, den], axis=0)

    def swap(n, buf, devs):
        for i, to in enumerate(devs):
            send(part.at[n], buf.at[i], t_s.at[8 * n + i], t_r.at[8 * n + i], to)

    def add(n, buf):
        acc = part[n]
        for i in range(7):
            got(buf.at[i], t_r.at[8 * n + i])
            acc = acc + buf[i]
        part[n + 1] = acc

    swap(0, x_in, [device(wrap(x + d // 2, X), y, z, wrap(c + d, 2)) for d in range(1, 8)])

    num0, den0 = jnp.sum(num), jnp.sum(den)
    theta0 = jnp.where(den0 > 0.0, num0 / jnp.where(den0 > 0.0, den0, 1.0), 0.0)

    def go_home(k, src, dst, n):
        to = device((x, xr)[k], y, z, hcore)
        if k == 0:
            send(src.at[0], dst.at[c], h_s.at[n, 0], h_r.at[n, c], to, when=jnp.logical_not(own_v))
            cp = pltpu.make_async_copy(src.at[0], dst.at[c], local.at[4 + n])
            pl.when(own_v)(lambda: cp.start())
        else:
            send(src.at[1], dst.at[c], h_s.at[n, 1], h_r.at[n, c], to)

    def got_home(dst, n):
        for k in (0, 1):
            keep = jnp.logical_and(own_v, c == k)
            got(dst.at[k], h_r.at[n, k], when=jnp.logical_not(keep))
            cp = pltpu.make_async_copy(dst.at[k], dst.at[k], local.at[4 + n])
            pl.when(keep)(lambda: cp.wait())

    for k in (0, 1):
        s1[k, pl.ds(0, BLK)] = first[k]
        s1[k, pl.ds(BLK, 8)] = jnp.full((8, BLK), theta0, jnp.float32)
        go_home(k, s1, s1h, 0)

    corr = jnp.concatenate([(first_b[k] - theta0 * v[k]).astype(jnp.bfloat16) for k in (0, 1)], axis=1)

    def left_loop(i, carry):
        left(i, corr)
        return carry

    lax.fori_loop(0, 8, left_loop, 0)
    add(0, x_in)
    swap(1, y_in, [device(x, wrap(y + d, Y), z, c) for d in (4, 3, 5, 2, 6, 1, 7)])
    total2 = lax.fori_loop(0, 8, right, zero)
    for k in (0, 1):
        g[k] = jnp.where(masks[k], total2[k], 0.0)
        go_home(k, g, gh, 1)
    add(1, y_in)
    swap(2, z_in, [device(x, y, wrap(z + d, Z), c) for d in (4, 3, 5, 2, 6, 1, 7)])

    got_home(s1h, 0)
    got_home(gh, 1)
    for k in (0, 1):
        out1[pl.ds(BLK * k, BLK)] = s1h[k, pl.ds(0, BLK)].astype(jnp.bfloat16)
    for cp, when in sent:
        if when is None:
            cp.wait_send()
        else:
            pl.when(when)(lambda cp=cp: cp.wait_send())
    add(2, z_in)
    theta = jnp.sum(part[3, pl.ds(0, 4)]) / jnp.sum(part[3, pl.ds(4, 4)])
    home_live = cols < sizes[4 * z + x]
    for k in (0, 1):
        mask = jnp.logical_and(rows < sizes[4 * y + 2 * c + k], home_live)
        shift = theta - s1h[k, BLK, 0]
        new = gh[k] - shift * s1h[k, pl.ds(0, BLK)]
        out2[pl.ds(BLK * k, BLK)] = jnp.where(mask, new, 0.0).astype(jnp.bfloat16)


def shards(wavefunction, left_env, right_env, sector_size):
    left = left_env.reshape(2, BLK, BLK)
    right = right_env.reshape(2, BLK, BLK)
    bf, f32 = jnp.bfloat16, jnp.float32
    hbm = pl.BlockSpec(memory_space=pltpu.MemorySpace.HBM)
    vmem = pl.BlockSpec(memory_space=pltpu.VMEM)
    dma = pltpu.SemaphoreType.DMA
    out = jax.ShapeDtypeStruct((2 * BLK, BLK), bf)
    return pl.pallas_call(
        kernel,
        out_shape=(out, out),
        in_specs=[hbm, hbm, hbm, hbm],
        out_specs=(vmem, vmem),
        scratch_shapes=[
            pltpu.SMEM((32,), jnp.int32),
            pltpu.VMEM((2 * BLK, BLK), bf),
            pltpu.VMEM((2, BLK, BLK), bf),
            pltpu.VMEM((2, 32, BLK, BLK), bf),
            pltpu.VMEM((2, 32, BLK, BLK), bf),
            pltpu.VMEM((2, BLK, BLK), bf),
            pltpu.VMEM((32, BLK, 2 * BLK), bf),
            pltpu.VMEM((2, BLK + 8, BLK), f32),
            pltpu.VMEM((2, BLK, BLK), f32),
            pltpu.VMEM((2, BLK + 8, BLK), f32),
            pltpu.VMEM((2, BLK, BLK), f32),
            pltpu.VMEM((4, 8, BLK), f32),
            pltpu.VMEM((7, 8, BLK), f32),
            pltpu.VMEM((7, 8, BLK), f32),
            pltpu.VMEM((7, 8, BLK), f32),
            dma((6,)),
            dma((9,)), dma((9,)), dma((8,)), dma((8,)), dma((2, 8)), dma((2, 8)),
            dma((1,)), dma((1,)), dma((9,)), dma((9,)), dma((8,)), dma((8, 2)), dma((8,)), dma((8,)),
            dma((2,)), dma((2,)), dma((2, 2)), dma((2, 2)), dma((24,)), dma((24,)),
        ],
        compiler_params=pltpu.CompilerParams(
            collective_id=0, has_side_effects=True, vmem_limit_bytes=60 << 20
        ),
        name="davidson",
    )(sector_size, wavefunction, left, right)


def solution(mesh):
    return jax.shard_map(
        shards,
        mesh=mesh,
        in_specs=(
            P("terms", "sectors"),
            P("terms", "sectors", None, None),
            P("terms", "sectors", None, None),
            P(),
        ),
        out_specs=(P("terms", "sectors"), P("terms", "sectors")),
        check_vma=False,
    )
```

time: 63.3 us -> 60.9 us (0.962)
  local copies, waits for them, and re-layouts: 4.43 us -> 2.14 us
    unnamed x10 -> x4, local copies, waits for them, and re-layouts: 4.43 us -> 2.14 us
where the time goes in v3:
time: 60.9 us; the launch traced here: 60.2 us
  Pallas kernels  57.4 us (94%)
  local copies, waits for them, and re-layouts  2.14 us (4%)
  between operations  0.65 us (1%)
    pallas_call x1, Pallas kernels, shards(): pl.pallas_call(kernel, out_shape=(out, out), in_specs=[hbm, hbm, hbm, hbm...  57.4 us
    unnamed x4, local copies, waits for them, and re-layouts  2.14 us

profile of v3, /device:TPU:6, one launch (start us, length us, event | category | flops | bytes accessed | tf_op | source)
XLA Modules:
  0.0 60.2 jit_solution(11114710955859892879)
XLA Ops:
  0.6 57.4 %davidson.1 = (bf16[256,128]{1,0:T(8,128)(2,1)}, bf16[256,128]{1,0:T(8,128)(2,1)}) custom-call(s32[32]{0:T(128)} %size_hbm.1, bf16[256,128]{1,0:T(8,128)(2,1)} %v_hbm.1, bf16[2,128,128]{2,1,0:T(8,128)(2,1)} %bitcast.2, bf16[2,128,128]{2,1,0:T(8,128)(2,1)} %bitcast.3), custom_call_target="tpu_custom_call" | custom-call | tf_op jit(solution)/shard_map/davidson/pallas_call | solution.py:358
  58.1 0.0 copy-start
  58.1 1.5 %copy.8 = bf16[256,128]{1,0:T(8,128)(2,1)} copy(bf16[256,128]{1,0:T(8,128)(2,1)} %get-tuple-element.4) | data formatting | bytes 131072
  59.6 0.0 copy-done
  59.6 0.6 %copy.9 = bf16[256,128]{1,0:T(8,128)(2,1)} copy(bf16[256,128]{1,0:T(8,128)(2,1)S(1)} %copy-done) | data formatting | bytes 131072
Async XLA Ops:
  58.1 1.5 %copy-start = (bf16[256,128]{1,0:T(8,128)(2,1)S(1)}, bf16[256,128]{1,0:T(8,128)(2,1)}, u32[]{:S(2)}) copy-start(bf16[256,128]{1,0:T(8,128)(2,1)} %get-tuple-element.5) | copy-start | bytes 196612

commit v4 on v3

--- a/solution.py
+++ b/solution.py
@@ -22,7 +22,7 @@
 
 
 def kernel(
-    size_hbm, v_hbm, l_hbm, r_hbm, out1, out2,
+    size_hbm, v_hbm, l_hbm, r_hbm, out,
     sizes, v_own, l_own, rb, ls, vc, im, s1, g, s1h, gh, part, x_in, y_in, z_in,
     local, ry_s, ry_r, rx_s, rx_r, rd_s, rd_r,
     la_s, la_r, lz_s, lz_r, lx_s, lx_r, ld_s, ld_r, v_s, v_r, h_s, h_r, t_s, t_r,
@@ -200,22 +200,22 @@
     do_r(1)
     do_r(2)
     beyond(0)
+    do_l(0)
     do_r(3)
     do_r(4)
     beyond(1)
     beyond(2)
-    do_l(0)
     do_r(5)
     do_r(6)
     beyond(3)
     beyond(4)
+    do_l(1)
+    do_l(2)
     do_r(7)
+    do_l(3)
+    do_l(4)
     beyond(5)
     beyond(6)
-    do_l(1)
-    do_l(2)
-    do_l(3)
-    do_l(4)
     beyond(7)
     do_l(5)
     do_l(6)
@@ -331,20 +331,21 @@
     got_home(s1h, 0)
     got_home(gh, 1)
     for k in (0, 1):
-        out1[pl.ds(BLK * k, BLK)] = s1h[k, pl.ds(0, BLK)].astype(jnp.bfloat16)
+        out[pl.ds(BLK * k, BLK)] = s1h[k, pl.ds(0, BLK)]
     for cp, when in sent:
         if when is None:
             cp.wait_send()
         else:
             pl.when(when)(lambda cp=cp: cp.wait_send())
     add(2, z_in)
-    theta = jnp.sum(part[3, pl.ds(0, 4)]) / jnp.sum(part[3, pl.ds(4, 4)])
+    sums = part[3]
+    theta = jnp.sum(sums[:4], keepdims=True) / jnp.sum(sums[4:], keepdims=True)
     home_live = cols < sizes[4 * z + x]
     for k in (0, 1):
         mask = jnp.logical_and(rows < sizes[4 * y + 2 * c + k], home_live)
-        shift = theta - s1h[k, BLK, 0]
+        shift = theta - s1h[k, pl.ds(BLK, 1)]
         new = gh[k] - shift * s1h[k, pl.ds(0, BLK)]
-        out2[pl.ds(BLK * k, BLK)] = jnp.where(mask, new, 0.0).astype(jnp.bfloat16)
+        out[pl.ds(BLK * (k + 2), BLK)] = jnp.where(mask, new, 0.0)
 
 
 def shards(wavefunction, left_env, right_env, sector_size):
@@ -354,12 +355,11 @@
     hbm = pl.BlockSpec(memory_space=pltpu.MemorySpace.HBM)
     vmem = pl.BlockSpec(memory_space=pltpu.VMEM)
     dma = pltpu.SemaphoreType.DMA
-    out = jax.ShapeDtypeStruct((2 * BLK, BLK), bf)
-    return pl.pallas_call(
+    wide = pl.pallas_call(
         kernel,
-        out_shape=(out, out),
+        out_shape=jax.ShapeDtypeStruct((4 * BLK, BLK), f32),
         in_specs=[hbm, hbm, hbm, hbm],
-        out_specs=(vmem, vmem),
+        out_specs=vmem,
         scratch_shapes=[
             pltpu.SMEM((32,), jnp.int32),
             pltpu.VMEM((2 * BLK, BLK), bf),
@@ -386,6 +386,7 @@
         ),
         name="davidson",
     )(sector_size, wavefunction, left, right)
+    return wide[: 2 * BLK].astype(bf), wide[2 * BLK :].astype(bf)
 
 
 def solution(mesh):

time: 60.9 us -> 58.6 us (0.962)
  local copies, waits for them, and re-layouts: 2.14 us -> 0.66 us
  Pallas kernels: 57.4 us -> 56.2 us
  other arithmetic: 0 us -> 0.97 us
    unnamed x4 -> x0, local copies, waits for them, and re-layouts: 2.14 us -> none
    pallas_call x1, Pallas kernels: 57.4 us -> 56.2 us  [shards(): pl.pallas_call(kernel, out_shape=jax.ShapeDtypeStruct((4 * BLK, BLK), f32...]
    another operation x0 -> x1, other arithmetic: none -> 0.97 us
    slice x0 -> x1, local copies, waits for them, and re-layouts: none -> 0.66 us  [shards(): return (wide[:2 * BLK].astype(bf), wide[2 * BLK:].astype(bf))]
where the time goes in v4:
time: 58.6 us; the launch traced here: 58.5 us
  Pallas kernels  56.2 us (96%)
  other arithmetic  0.97 us (2%)
  local copies, waits for them, and re-layouts  0.66 us (1%)
  between operations  0.64 us (1%)
    pallas_call x1, Pallas kernels, shards(): pl.pallas_call(kernel, out_shape=jax.ShapeDtypeStruct((4 * BLK, BLK), f32...  56.2 us

profile of v4, /device:TPU:6, one launch (start us, length us, event | category | flops | bytes accessed | tf_op | source)
XLA Modules:
  0.0 58.5 jit_solution(11227871551760845752)
XLA Ops:
  0.6 56.2 %davidson.1 = f32[512,128]{1,0:T(8,128)} custom-call(s32[32]{0:T(128)} %size_hbm.1, bf16[256,128]{1,0:T(8,128)(2,1)} %v_hbm.1, bf16[2,128,128]{2,1,0:T(8,128)(2,1)} %bitcast.2, bf16[2,128,128]{2,1,0:T(8,128)(2,1)} %bitcast.3), custom_call_target="tpu_custom_call" | custom-call | tf_op jit(solution)/shard_map/davidson/pallas_call | solution.py:358
  56.8 1.0 %convert.4 = bf16[512,128]{1,0:T(8,128)(2,1)S(1)} convert(f32[512,128]{1,0:T(8,128)} %davidson.1) | non-fusion elementwise | flops 65536 | bytes 393216 | tf_op jit(solution)/shard_map/convert.1
  57.8 0.7 %fusion = (bf16[256,128]{1,0:T(8,128)(2,1)}, bf16[256,128]{1,0:T(8,128)(2,1)}) fusion(bf16[512,128]{1,0:T(8,128)(2,1)S(1)} %convert.4), kind=kLoop, calls=%fused_computation | loop fusion | bytes 262144 | tf_op jit(solution)/shard_map/slice | solution.py:389

commit v5 on v4

--- a/solution.py
+++ b/solution.py
@@ -202,8 +202,8 @@
     beyond(0)
     do_l(0)
     do_r(3)
+    beyond(1)
     do_r(4)
-    beyond(1)
     beyond(2)
     do_r(5)
     do_r(6)
@@ -216,9 +216,9 @@
     do_l(4)
     beyond(5)
     beyond(6)
-    beyond(7)
     do_l(5)
     do_l(6)
+    beyond(7)
     do_l(7)
 
     got(vc.at[0], v_r.at[0], when=jnp.logical_not(own_v))

time: 58.6 us -> 57.9 us (0.988); the launches traced: 58.5 us -> 57.1 us
  Pallas kernels: 56.2 us -> 54.8 us
    pallas_call x1, Pallas kernels: 56.2 us -> 54.8 us  [shards(): pl.pallas_call(kernel, out_shape=jax.ShapeDtypeStruct((4 * BLK, BLK), f32...]
where the time goes in v5:
time: 57.9 us; the launch traced here: 57.1 us
  Pallas kernels  54.8 us (95%)
  other arithmetic  0.97 us (2%)
  local copies, waits for them, and re-layouts  0.66 us (1%)
  between operations  0.64 us (1%)
    pallas_call x1, Pallas kernels, shards(): pl.pallas_call(kernel, out_shape=jax.ShapeDtypeStruct((4 * BLK, BLK), f32...  54.8 us

profile of v5, /device:TPU:6, one launch (start us, length us, event | category | flops | bytes accessed | tf_op | source)
XLA Modules:
  0.0 57.1 jit_solution(8683995874959797821)
XLA Ops:
  0.6 54.8 %davidson.1 = f32[512,128]{1,0:T(8,128)} custom-call(s32[32]{0:T(128)} %size_hbm.1, bf16[256,128]{1,0:T(8,128)(2,1)} %v_hbm.1, bf16[2,128,128]{2,1,0:T(8,128)(2,1)} %bitcast.2, bf16[2,128,128]{2,1,0:T(8,128)(2,1)} %bitcast.3), custom_call_target="tpu_custom_call" | custom-call | tf_op jit(solution)/shard_map/davidson/pallas_call | solution.py:358
  55.5 1.0 %convert.4 = bf16[512,128]{1,0:T(8,128)(2,1)S(1)} convert(f32[512,128]{1,0:T(8,128)} %davidson.1) | non-fusion elementwise | flops 65536 | bytes 393216 | tf_op jit(solution)/shard_map/convert.1
  56.4 0.7 %fusion = (bf16[256,128]{1,0:T(8,128)(2,1)}, bf16[256,128]{1,0:T(8,128)(2,1)}) fusion(bf16[512,128]{1,0:T(8,128)(2,1)S(1)} %convert.4), kind=kLoop, calls=%fused_computation | loop fusion | bytes 262144 | tf_op jit(solution)/shard_map/slice | solution.py:389

commit v6 on v5

--- a/solution.py
+++ b/solution.py
@@ -206,15 +206,15 @@
     do_r(4)
     beyond(2)
     do_r(5)
+    beyond(3)
     do_r(6)
-    beyond(3)
     beyond(4)
     do_l(1)
     do_l(2)
     do_r(7)
+    beyond(5)
     do_l(3)
     do_l(4)
-    beyond(5)
     beyond(6)
     do_l(5)
     do_l(6)

time: 57.9 us -> 58.1 us (level)
  Pallas kernels: 54.8 us -> 55.6 us
    pallas_call x1, Pallas kernels: 54.8 us -> 55.6 us  [shards(): pl.pallas_call(kernel, out_shape=jax.ShapeDtypeStruct((4 * BLK, BLK), f32...]
where the time goes in v6:
time: 58.1 us; the launch traced here: 57.9 us
  Pallas kernels  55.6 us (96%)
  other arithmetic  0.97 us (2%)
  local copies, waits for them, and re-layouts  0.66 us (1%)
  between operations  0.64 us (1%)
    pallas_call x1, Pallas kernels, shards(): pl.pallas_call(kernel, out_shape=jax.ShapeDtypeStruct((4 * BLK, BLK), f32...  55.6 us

profile of v6, /device:TPU:6, one launch (start us, length us, event | category | flops | bytes accessed | tf_op | source)
XLA Modules:
  0.0 57.9 jit_solution(6231668586761774380)
XLA Ops:
  0.6 55.6 %davidson.1 = f32[512,128]{1,0:T(8,128)} custom-call(s32[32]{0:T(128)} %size_hbm.1, bf16[256,128]{1,0:T(8,128)(2,1)} %v_hbm.1, bf16[2,128,128]{2,1,0:T(8,128)(2,1)} %bitcast.2, bf16[2,128,128]{2,1,0:T(8,128)(2,1)} %bitcast.3), custom_call_target="tpu_custom_call" | custom-call | tf_op jit(solution)/shard_map/davidson/pallas_call | solution.py:358
  56.3 1.0 %convert.4 = bf16[512,128]{1,0:T(8,128)(2,1)S(1)} convert(f32[512,128]{1,0:T(8,128)} %davidson.1) | non-fusion elementwise | flops 65536 | bytes 393216 | tf_op jit(solution)/shard_map/convert.1
  57.2 0.7 %fusion = (bf16[256,128]{1,0:T(8,128)(2,1)}, bf16[256,128]{1,0:T(8,128)(2,1)}) fusion(bf16[512,128]{1,0:T(8,128)(2,1)S(1)} %convert.4), kind=kLoop, calls=%fused_computation | loop fusion | bytes 262144 | tf_op jit(solution)/shard_map/slice | solution.py:389
